TPU v7x, 32 devices: a whole 2x2x4 slice. The times are simulated.
32 devices in a mesh: rep: 2 (over y), grp: 4 (over x, core), loc: 4 (over z).
Axes of the slice: x: 2, y: 2, z: 4, core: 2. Of those that a mesh axis runs over, the one named last changes fastest.
Arguments:
- tokens: bfloat16 [256, 7168], P(('rep', 'grp', 'loc')), parts along dimension 0, may hold values from -6 to 6
- expert_ids: int32 [256, 8], P(('rep', 'grp', 'loc')), parts along dimension 0, may hold values from 0 to 15, as said below
- gate_values: bfloat16 [256, 8], P(('rep', 'grp', 'loc')), parts along dimension 0, may hold values from 0.049804688 to 0.59765625
- w_gate: bfloat16 [16, 7168, 1024], P(('grp', 'loc')), may hold values from -0.0625 to 0.0625
- w_up: bfloat16 [16, 7168, 1024], P(('grp', 'loc')), may hold values from -0.0625 to 0.0625
- w_down: bfloat16 [16, 1024, 7168], P(('grp', 'loc')), may hold values from -0.1875 to 0.1875
Outputs:
- mixed: bfloat16 [256, 7168], P(('rep', 'grp', 'loc')), parts along dimension 0
There are 2 independent parts, one for each index of `rep`. A program takes and returns all parts, laid end to end along the dimension named above; an argument that names none is the same for every part. Nothing has to cross between parts.
Inputs may be any that keep to these rules, and one draw needn't show every extreme that they name: `expert_ids`: each row names 8 distinct experts, 2 in each of 4 distinct node groups, group g holding experts g * 4 to (g + 1) * 4 - 1. The rows of one device (aligned blocks of 8 rows) name any one expert at most 4 times. In every draw one group is named by every row, and each of its experts exactly 4 times by the rows of every device.
All inputs are finite; a program needn't handle non-finite values.
Results may differ from a plain program's by a relative error of at most 0.0065.
Values may be sent and summed in bfloat16 or wider, within the bound.
A program may use at most 128 MiB of HBM per device.

v0:
```python
import jax
import jax.numpy as jnp
from jax import lax
from jax.sharding import PartitionSpec as P

GSEL = 4
EXP_GROUP = 4


def expert_rows(rows, gates, w_gate, w_up, w_down):
    shape = rows.shape
    flat = rows.reshape(-1, shape[-1])
    gate_part = jnp.dot(flat, w_gate[0], preferred_element_type=jnp.float32)
    up_part = jnp.dot(flat, w_up[0], preferred_element_type=jnp.float32)
    hidden = (jax.nn.silu(gate_part) * up_part).astype(jnp.bfloat16)
    down = jnp.dot(hidden, w_down[0], preferred_element_type=jnp.float32)
    down = down * gates.reshape(-1, 1).astype(jnp.float32)
    return down.astype(jnp.bfloat16).reshape(shape)


def body(tokens, expert_ids, gate_values, w_gate, w_up, w_down):
    rows, width = tokens.shape
    topk = expert_ids.shape[1]
    n_grp = lax.axis_size("grp")
    n_loc = lax.axis_size("loc")
    per_group = topk // GSEL
    split = n_loc // EXP_GROUP
    cap_own = per_group * rows // EXP_GROUP
    group_of = expert_ids // EXP_GROUP
    owner_of = expert_ids % EXP_GROUP
    groups_idx = jnp.arange(n_grp, dtype=jnp.int32)
    token_idx = jnp.arange(rows, dtype=jnp.int32)
    member = jnp.any(group_of[:, :, None] == groups_idx[None, None, :], axis=1)
    member_int = member.astype(jnp.int32)
    slot_one = jnp.cumsum(member_int, axis=0) - member_int
    target_one = jnp.where(member, groups_idx[None, :] * rows + slot_one, n_grp * rows)
    owners_of_slot = jnp.broadcast_to(token_idx[:, None], (rows, n_grp)).reshape(-1)
    source_one = (
        jnp.full((n_grp * rows,), rows, jnp.int32)
        .at[target_one.reshape(-1)]
        .set(owners_of_slot, mode="drop")
    )
    valid_one = source_one < rows
    safe_one = jnp.minimum(source_one, rows - 1)
    send_rows = jnp.where(
        valid_one[:, None], tokens[safe_one], jnp.zeros((), jnp.bfloat16)
    ).reshape(n_grp, rows, width)
    group_hot = (group_of[:, :, None] == groups_idx[None, None, :]).astype(jnp.float32)
    owner_hot = (
        owner_of[:, :, None] == jnp.arange(EXP_GROUP, dtype=jnp.int32)[None, None, :]
    ).astype(jnp.float32)
    weighted = group_hot * gate_values.astype(jnp.float32)[:, :, None]
    dense = jnp.einsum("tkg,tko->tgo", weighted, owner_hot, precision=lax.Precision.HIGHEST)
    dense = jnp.repeat(dense, split, axis=2)
    dense_slots = dense[safe_one.reshape(n_grp, rows), groups_idx[:, None], :]
    send_gates = jnp.where(valid_one.reshape(n_grp, rows)[:, :, None], dense_slots, 0.0).astype(
        jnp.bfloat16
    )
    arrived_rows, arrived_gates = (
        lax.all_to_all(send_rows, "grp", split_axis=0, concat_axis=0, tiled=True),
        lax.all_to_all(send_gates, "grp", split_axis=0, concat_axis=0, tiled=True),
    )
    live = arrived_gates > 0
    live_int = live.astype(jnp.int32)
    rank_two = jnp.cumsum(live_int, axis=1) - live_int
    cap_two = n_grp * cap_own
    owner_axis = jnp.arange(n_loc, dtype=jnp.int32)[None, None, :]
    target_two = jnp.where(
        live, owner_axis * cap_two + groups_idx[:, None, None] * cap_own + rank_two, n_loc * cap_two
    )
    slot_index = jnp.broadcast_to(
        groups_idx[:, None, None] * rows + token_idx[None, :, None], (n_grp, rows, n_loc)
    )
    source_two = (
        jnp.full((n_loc * cap_two,), n_grp * rows, jnp.int32)
        .at[target_two.reshape(-1)]
        .set(slot_index.reshape(-1), mode="drop")
    )
    valid_two = source_two < n_grp * rows
    safe_two = jnp.minimum(source_two, n_grp * rows - 1)
    flat_arrived = arrived_rows.reshape(n_grp * rows, width)
    fwd_rows = jnp.where(
        valid_two[:, None], flat_arrived[safe_two], jnp.zeros((), jnp.bfloat16)
    ).reshape(n_loc, cap_two, width)
    owner_column = jnp.arange(n_loc * cap_two, dtype=jnp.int32) // cap_two
    fwd_gates = jnp.where(
        valid_two,
        arrived_gates.reshape(n_grp * rows, n_loc)[safe_two, owner_column],
        jnp.zeros((), jnp.bfloat16),
    ).reshape(n_loc, cap_two)
    outputs = expert_rows(
        lax.all_to_all(fwd_rows, "loc", split_axis=0, concat_axis=0, tiled=True),
        lax.all_to_all(fwd_gates, "loc", split_axis=0, concat_axis=0, tiled=True),
        w_gate,
        w_up,
        w_down,
    )
    back_two = lax.all_to_all(outputs, "loc", split_axis=0, concat_axis=0, tiled=True)
    partial_value = (
        jnp.zeros((n_grp * rows, width), jnp.float32)
        .at[safe_two]
        .add(back_two.reshape(-1, width).astype(jnp.float32))
    )
    back_one = lax.all_to_all(
        partial_value.astype(jnp.bfloat16).reshape(n_grp, rows, width),
        "grp",
        split_axis=0,
        concat_axis=0,
        tiled=True,
    )
    flat_back = back_one.reshape(n_grp * rows, width)
    pick = jnp.where(member, groups_idx[None, :] * rows + slot_one, 0)
    gathered = flat_back[pick.reshape(-1)].reshape(rows, n_grp, width)
    result = jnp.einsum(
        "tg,tgd->td", member.astype(jnp.bfloat16), gathered, preferred_element_type=jnp.float32
    )
    return result.astype(jnp.bfloat16)


def solution(mesh):
    placed = (
        P(("rep", "grp", "loc"), None),
        P(("rep", "grp", "loc"), None),
        P(("rep", "grp", "loc"), None),
        P(("grp", "loc"), None, None),
        P(("grp", "loc"), None, None),
        P(("grp", "loc"), None, None),
    )
    return jax.shard_map(
        body, mesh=mesh, in_specs=placed, out_specs=P(("rep", "grp", "loc"), None), check_vma=False
    )
```

profile of v0, /device:TPU:0, one launch (start us, length us, event | category | flops | bytes accessed | tf_op | source)
XLA Modules:
  0.0 124.9 jit_solution(14832335598991852304)
XLA Ops:
  0.0 0.0 copy-start
  0.0 0.7 add_select_fusion.2
  0.7 0.2 fusion.31
  1.0 0.1 reduce_or.12
  1.1 0.1 reduce_window_sum.25
  1.2 0.1 add.159
  1.3 0.1 reshape.385
  1.4 0.7 scatter_custom_fusion
  2.1 0.1 reshape.333
  2.2 0.1 reshape.345
  2.2 0.7 convert_element_type.61
  2.9 0.2 fusion.29
  3.1 0.7 gather_fusion
  3.8 0.1 copy.18
  3.9 0.1 broadcast_in_dim.104
  4.0 0.6 copy.12
  4.6 4.2 %all-to-all-start = ((bf16[4,8,4]{1,2,0:T(4,128)(2,1)}), bf16[4,8,4]{1,2,0:T(4,128)(2,1)S(1)}, u32[]{:S(2)}, u32[]{:S(2)}) async-start(bf16[4,8,4]{1,2,0:T(4,128)(2,1)} %copy.12), calls=%async_computation | async-start | bytes 8192 | tf_op jit(solution)/shard_map/all_to_all | solution.py:61
  8.8 0.0 copy-done
  8.8 0.8 gather_fusion.1
  9.7 0.9 bitcast_select_fusion
  10.5 0.1 broadcast_add_fusion
  10.6 0.1 iota_add_fusion
  10.7 0.1 broadcast_in_dim.109
  10.8 0.1 reshape.393
  10.9 1.7 %all-to-all-done = bf16[4,8,4]{1,2,0:T(4,128)(2,1)S(1)} async-done(((bf16[4,8,4]{1,2,0:T(4,128)(2,1)}), bf16[4,8,4]{1,2,0:T(4,128)(2,1)S(1)}, u32[]{:S(2)}, u32[]{:S(2)}) %all-to-all-start) | async-done | bytes 288 | tf_op jit(solution)/shard_map/all_to_all | solution.py:61
  12.6 3.5 %all-to-all-start.1 = ((bf16[4,8,7168]{2,1,0:T(8,128)(2,1)}), bf16[4,8,7168]{2,1,0:T(8,128)(2,1)S(1)}, u32[]{:S(2)}, u32[]{:S(2)}) async-start(bf16[4,8,7168]{2,1,0:T(8,128)(2,1)} %bitcast_select_fusion), calls=%async_computation.1 | async-start | bytes 917504 | tf_op jit(solution)/shard_map/all_to_all | solution.py:60
  16.1 0.7 reduce_window_sum.26
  16.8 0.1 add_select_fusion
  16.9 0.1 copy.13
  17.0 0.1 reshape.334
  17.1 1.0 scatter_custom_fusion.1
  18.1 0.1 broadcast_in_dim.111
  18.2 0.1 reshape.338
  18.3 0.9 gather_fusion.3
  19.2 0.7 all_to_all.28
  19.9 4.3 %all-to-all-done.1 = bf16[4,8,7168]{2,1,0:T(8,128)(2,1)S(1)} async-done(((bf16[4,8,7168]{2,1,0:T(8,128)(2,1)}), bf16[4,8,7168]{2,1,0:T(8,128)(2,1)S(1)}, u32[]{:S(2)}, u32[]{:S(2)}) %all-to-all-start.1) | async-done | bytes 458784 | tf_op jit(solution)/shard_map/all_to_all | solution.py:60
  24.2 5.3 %all-to-all-start.3 = ((bf16[4,1,16]{2,1,0:T(2,128)(2,1)}), bf16[4,1,16]{2,1,0:T(2,128)(2,1)S(1)}, u32[]{:S(2)}, u32[]{:S(2)}) async-start(bf16[4,1,16]{2,1,0:T(2,128)(2,1)} %all_to_all.28), calls=%async_computation.3 | async-start | bytes 4096 | tf_op jit(solution)/shard_map/all_to_all | solution.py:93
  29.5 1.1 gather_fusion.2
  30.6 1.1 broadcast_select_fusion
  31.7 3.3 %all-to-all-done.3 = bf16[4,1,16]{2,1,0:T(2,128)(2,1)S(1)} async-done(((bf16[4,1,16]{2,1,0:T(2,128)(2,1)}), bf16[4,1,16]{2,1,0:T(2,128)(2,1)S(1)}, u32[]{:S(2)}, u32[]{:S(2)}) %all-to-all-start.3) | async-done | bytes 160 | tf_op jit(solution)/shard_map/all_to_all | solution.py:93
  35.0 3.5 %all-to-all-start.2 = ((bf16[4,16,7168]{2,1,0:T(8,128)(2,1)}), bf16[4,16,7168]{2,1,0:T(8,128)(2,1)S(1)}, u32[]{:S(2)}, u32[]{:S(2)}) async-start(bf16[4,16,7168]{2,1,0:T(8,128)(2,1)} %broadcast_select_fusion), calls=%async_computation.2 | async-start | bytes 1835008 | tf_op jit(solution)/shard_map/all_to_all | solution.py:92
  38.5 0.1 reshape.343
  38.6 21.4 %all-to-all-done.2 = bf16[4,16,7168]{2,1,0:T(8,128)(2,1)S(1)} async-done(((bf16[4,16,7168]{2,1,0:T(8,128)(2,1)}), bf16[4,16,7168]{2,1,0:T(8,128)(2,1)S(1)}, u32[]{:S(2)}, u32[]{:S(2)}) %all-to-all-start.2) | async-done | bytes 917536 | tf_op jit(solution)/shard_map/all_to_all | solution.py:92
  60.0 7.8 %fusion.4 = f32[64,1024]{1,0:T(8,128)S(1)} fusion(bf16[64,7168]{1,0:T(8,128)(2,1)S(1)} %bitcast.54, bf16[1,7168,1024]{2,1,0:T(8,128)(2,1)} %param.9), kind=kOutput, calls=%fused_computation.12 | convolution fusion | flops 939524096 | bytes 15859712 | tf_op jit(solution)/shard_map/dot_general | solution.py:13
  67.8 14.6 %fusion.9 = bf16[64,7168]{1,0:T(8,128)(2,1)S(1)} fusion(bf16[1,1024,7168]{2,1,0:T(8,128)(2,1)} %param.11, f32[64]{0:T(128)S(1)} %reshape.343, bf16[64,7168]{1,0:T(8,128)(2,1)S(1)} %bitcast.55, bf16[1,7168,1024]{2,1,0:T(8,128)(2,1)} %param.10, f32[64,1024]{1,0:T(8,128)S(1)} %fusion.4), kind=kOutput, calls=%fused_computation.15 | convolution fusion | flops 1880358912 | bytes 31457536 | tf_op jit(solution)/shard_map/dot_general | solution.py:16
  82.4 24.9 %all_to_all.35 = bf16[4,16,7168]{2,1,0:T(8,128)(2,1)S(1)} all-to-all(bf16[4,16,7168]{2,1,0:T(8,128)(2,1)S(1)} %bitcast.58), channel_id=1, replica_groups=mesh['rep'=2,'grp'=4,'loc'=4] {'loc'}, dimensions={0} | all-to-all | bytes 1835008 | tf_op jit(solution)/shard_map/all_to_all | solution.py:98
  107.3 3.1 %scatter_custom_fusion.2 = f32[32,7168]{1,0:T(8,128)S(1)} fusion(s32[64]{0:T(128)S(1)} %get-tuple-element.6, bf16[64,7168]{1,0:T(8,128)(2,1)S(1)} %bitcast.57, f32[]{:T(128)} %constant.77.clone.1), kind=kCustom, calls=%fused_computation.16 | custom fusion | flops 917504 | bytes 1835012 | tf_op jit(solution)/shard_map/scatter-add | solution.py:102
  110.4 0.8 convert_bitcast_fusion
  111.2 3.5 %all-to-all-start.5 = ((bf16[4,8,7168]{2,1,0:T(8,128)(2,1)}), bf16[4,8,7168]{2,1,0:T(8,128)(2,1)S(1)}, u32[]{:S(2)}, u32[]{:S(2)}) async-start(bf16[4,8,7168]{2,1,0:T(8,128)(2,1)} %convert_bitcast_fusion), calls=%async_computation.5 | async-start | bytes 917504 | tf_op jit(solution)/shard_map/all_to_all | solution.py:104
  114.7 8.1 %all-to-all-done.5 = bf16[4,8,7168]{2,1,0:T(8,128)(2,1)S(1)} async-done(((bf16[4,8,7168]{2,1,0:T(8,128)(2,1)}), bf16[4,8,7168]{2,1,0:T(8,128)(2,1)S(1)}, u32[]{:S(2)}, u32[]{:S(2)}) %all-to-all-start.5) | async-done | bytes 458784 | tf_op jit(solution)/shard_map/all_to_all | solution.py:104
  122.8 0.8 gather_fusion.4
  123.6 0.2 reshape.342
  123.8 0.4 fusion.32
  124.2 0.7 copy.22
  (21 shorter events, 0.2 us)
Async XLA Ops:
  0.0 8.8 %copy-start = (bf16[8,7168]{1,0:T(8,128)(2,1)S(1)}, bf16[8,7168]{1,0:T(8,128)(2,1)}, u32[]{:S(2)}) copy-start(bf16[8,7168]{1,0:T(8,128)(2,1)} %param.6) | copy-start | bytes 344068
  4.6 8.0 %all-to-all-start = ((bf16[4,8,4]{1,2,0:T(4,128)(2,1)}), bf16[4,8,4]{1,2,0:T(4,128)(2,1)S(1)}, u32[]{:S(2)}, u32[]{:S(2)}) async-start(bf16[4,8,4]{1,2,0:T(4,128)(2,1)} %copy.12), calls=%async_computation | async-start | bytes 8192 | tf_op jit(solution)/shard_map/all_to_all | solution.py:61
  12.6 11.6 %all-to-all-start.1 = ((bf16[4,8,7168]{2,1,0:T(8,128)(2,1)}), bf16[4,8,7168]{2,1,0:T(8,128)(2,1)S(1)}, u32[]{:S(2)}, u32[]{:S(2)}) async-start(bf16[4,8,7168]{2,1,0:T(8,128)(2,1)} %bitcast_select_fusion), calls=%async_computation.1 | async-start | bytes 917504 | tf_op jit(solution)/shard_map/all_to_all | solution.py:60
  24.2 10.8 %all-to-all-start.3 = ((bf16[4,1,16]{2,1,0:T(2,128)(2,1)}), bf16[4,1,16]{2,1,0:T(2,128)(2,1)S(1)}, u32[]{:S(2)}, u32[]{:S(2)}) async-start(bf16[4,1,16]{2,1,0:T(2,128)(2,1)} %all_to_all.28), calls=%async_computation.3 | async-start | bytes 4096 | tf_op jit(solution)/shard_map/all_to_all | solution.py:93
  35.0 25.0 %all-to-all-start.2 = ((bf16[4,16,7168]{2,1,0:T(8,128)(2,1)}), bf16[4,16,7168]{2,1,0:T(8,128)(2,1)S(1)}, u32[]{:S(2)}, u32[]{:S(2)}) async-start(bf16[4,16,7168]{2,1,0:T(8,128)(2,1)} %broadcast_select_fusion), calls=%async_computation.2 | async-start | bytes 1835008 | tf_op jit(solution)/shard_map/all_to_all | solution.py:92
  111.2 11.6 %all-to-all-start.5 = ((bf16[4,8,7168]{2,1,0:T(8,128)(2,1)}), bf16[4,8,7168]{2,1,0:T(8,128)(2,1)S(1)}, u32[]{:S(2)}, u32[]{:S(2)}) async-start(bf16[4,8,7168]{2,1,0:T(8,128)(2,1)} %convert_bitcast_fusion), calls=%async_computation.5 | async-start | bytes 917504 | tf_op jit(solution)/shard_map/all_to_all | solution.py:104
where the time goes:
time: 125 us
  waiting for transfers between devices  38.8 us (31%)
  blocking collectives  24.9 us (20%)
  matrix products  23 us (18%)
  starting transfers between devices  20 us (16%)
  local copies, waits for them, and re-layouts  9.48 us (8%)
  other arithmetic  8.54 us (7%)
    all_to_all x1, blocking collectives, body(): lax.all_to_all(outputs, 'loc', split_axis=0, concat_axis=0, tiled=True)  24.9 us
    all_to_all x1, waiting for transfers between devices, body(): lax.all_to_all(fwd_rows, 'loc', split_axis=0, concat_axis=0, tiled=True)  21.4 us
    dot_general x1, matrix products, expert_rows(): down = jnp.dot(hidden, w_down[0], preferred_element_type=jnp.float32)  14.6 us
    all_to_all x1, waiting for transfers between devices, body(): lax.all_to_all(partial_value.astype(jnp.bfloat16).reshape(n_grp, rows, wi...  8.1 us
    dot_general x1, matrix products, expert_rows(): gate_part = jnp.dot(flat, w_gate[0], preferred_element_type=jnp.float32)  7.82 us
    all_to_all x1, starting transfers between devices, body(): lax.all_to_all(fwd_gates, 'loc', split_axis=0, concat_axis=0, tiled=True)  5.33 us
    all_to_all x1, waiting for transfers between devices, body(): lax.all_to_all(send_rows, 'grp', split_axis=0, concat_axis=0, tiled=True)  4.31 us
    all_to_all x1, starting transfers between devices, body(): lax.all_to_all(send_gates, 'grp', split_axis=0, concat_axis=0, tiled=True)  4.21 us
  transfers between devices with their start and end apart: 5, of which 5 were waited for; matrix products, arithmetic and copies ran while one was open for 6% of the time, Pallas kernels for 0%

commit v1 on v0

v1 whole, which is shorter than its diff:
```python
import functools

import jax
import jax.numpy as jnp
from jax import lax
from jax.experimental import pallas as pl
from jax.experimental.pallas import tpu as pltpu
from jax.sharding import PartitionSpec as P

EXP_GROUP = 4
LANES = 128
C_IN = 2
C_OUT = 4
F32 = jnp.float32
BF16 = jnp.bfloat16


def al(v, m):
    return pl.multiple_of(v, m)


def kernel(nx, nz, tok_ref, ids_ref, gv_ref, wg_hbm, wu_hbm, wd_hbm, out_ref,
           wg, wu, wd, pk, pk_in, gat, gts, acc_g, acc_u, hid, snd, tin, xin, zl, zr, zsl, zsr, res, fin, fin_in,
           w_sem, wd_sem, pk_sem, gts_s, gts_r, zs, zv, xs, xv, cs, cv, ss, sr, xos, xor, zos, zor, fs, fr):
    rows, width = tok_ref.shape
    half = width // 2
    blk = 2 * rows
    nb = nx * nz
    total = nb * blk
    wi = half // C_IN
    wo = half // C_OUT
    ff = wg.shape[1]
    g = lax.axis_index("grp")
    z = lax.axis_index("loc")
    x = g // 2
    c = g % 2
    other = 1 - c
    mate = x * 2 + other

    def rc(src, dst, s, r, grp=None, loc=None):
        return pltpu.make_async_remote_copy(
            src_ref=src, dst_ref=dst, send_sem=s, recv_sem=r,
            device_id={"grp": g if grp is None else grp, "loc": z if loc is None else loc},
            device_id_type=pl.DeviceIdType.MESH)

    def w_copy(i, k):
        src, dst = ((wg_hbm, wg), (wu_hbm, wu))[i]
        return pltpu.make_async_copy(src.at[0, pl.ds(k * wi, wi), :], dst.at[pl.ds(k * wi, wi), :], w_sem.at[i, k])

    def wd_copy(h, j):
        return pltpu.make_async_copy(
            wd_hbm.at[0, :, pl.ds(al(h * half + j * wo, LANES), wo)], wd.at[h * C_OUT + j], wd_sem.at[h * C_OUT + j])

    for j in range(C_IN):
        for h in range(2):
            for i in range(2):
                w_copy(i, h * C_IN + j).start()
    for j in range(C_OUT):
        wd_copy(other, j).start()
        wd_copy(c, j).start()

    barrier = pltpu.get_barrier_semaphore()

    def chips():
        for dx in range(nx):
            for dz in range(nz):
                if dx or dz:
                    yield dx * nz + dz - 1, lax.rem(x + dx, nx), lax.rem(z + dz, nz)

    pl.semaphore_signal(barrier, inc=1, device_id={"grp": mate, "loc": z}, device_id_type=pl.DeviceIdType.MESH)
    for _, xb, zb in chips():
        pl.semaphore_signal(barrier, inc=1, device_id={"grp": xb * 2 + c, "loc": zb},
                            device_id_type=pl.DeviceIdType.MESH)

    tok = tok_ref[...].astype(F32)
    lane = lax.broadcasted_iota(jnp.int32, (rows, LANES), 1)
    ids = ids_ref[...]
    gv = gv_ref[...].astype(F32)
    dense = jnp.zeros((rows, LANES), F32)
    for k in range(ids.shape[1]):
        dense = dense + jnp.where(lane == ids[:, k:k + 1], gv[:, k:k + 1], 0.0)
    pk[:, :half] = jnp.concatenate([tok[:, :half], tok[:, half:]], axis=0).astype(BF16)
    pk[:, half:] = jnp.concatenate([dense, dense], axis=0).astype(BF16)
    pl.semaphore_wait(barrier, nb)
    swap = rc(pk, pk_in, pk_sem.at[0], pk_sem.at[1], grp=mate)
    swap.start()

    def rows_of(xb, zb):
        return pl.ds(al((xb * nz + zb) * blk, blk), blk)

    swap.wait_recv()
    mine, theirs = pk[...].astype(F32), pk_in[...].astype(F32)
    a = jnp.where(c == 0, mine, theirs)
    b = jnp.where(c == 0, theirs, mine)
    for h in range(2):
        both = jnp.concatenate([a[h * rows:(h + 1) * rows, :half], b[h * rows:(h + 1) * rows, :half]], axis=0)
        both = both.astype(BF16)
        for j in range(C_IN):
            gat[h * C_IN + j, rows_of(x, z), :] = both[:, j * wi:(j + 1) * wi]
    gts[rows_of(x, z), :] = jnp.concatenate([a[:rows, half:], b[:rows, half:]], axis=0).astype(BF16)

    sends = []

    def go(cond, cp):
        sends.append((cond, cp))
        if cond is None:
            cp.start()
        else:
            pl.when(cond)(cp.start)

    def both_conds(p, q):
        return p if q is None else q if p is None else jnp.logical_and(p, q)

    def piece(h, j, xb, zb):
        return gat.at[h * C_IN + j, rows_of(xb, zb), :]

    def zcopy(way, j, d, zb):
        p = piece(c, j, x, zb)
        return rc(p, p, zs.at[way, j, d], zv.at[way, j, d], loc=z + 1 if way == 0 else z - 1)

    def xcopy(j, xd, slot, xb, zb, to):
        p = piece(c, j, xb, zb)
        return rc(p, p, xs.at[j, xd - 1, slot], xv.at[j, xd - 1, slot], grp=to * 2 + c)

    def ccopy(h, j, xd, slot, xb, zb):
        p = piece(h, j, xb, zb)
        return rc(p, p, cs.at[j, xd, slot], cv.at[j, xd, slot], grp=mate)

    can = (z + 1 < nz, z >= 1)

    def spread(cond, j, slot, zb):
        for xd in range(1, nx):
            go(cond, xcopy(j, xd, slot, x, zb, lax.rem(x + xd, nx)))

    for j in range(C_IN):
        for way in range(2):
            go(can[way], zcopy(way, j, 0, z))
        spread(None, j, 0, z)
    for n, xb, zb in chips():
        p = gts.at[rows_of(x, z), :]
        go(None, rc(p, p, gts_s.at[n], gts_r.at[n], grp=xb * 2 + c, loc=zb))

    def slots(d):
        if d == 0:
            return [(None, 0, z)]
        return [(z >= d, d, z - d), (z + d < nz, nz - 1 + d, z + d)]

    def x_arrivals(d, j):
        for cond, slot, zb in slots(d):
            for xd in range(1, nx):
                xb = lax.rem(x + nx - xd, nx)

                def take():
                    xcopy(j, xd, slot, xb, zb, x).wait_recv()
                    ccopy(c, j, xd, slot, xb, zb).start()
                if cond is None:
                    take()
                else:
                    pl.when(cond)(take)
                sends.append((cond, ccopy(c, j, xd, slot, xb, zb)))

    for d in range(1, nz):
        for j in range(C_IN):
            for way, (cond, slot, zb) in enumerate(slots(d)):
                pl.when(cond)(zcopy(way, j, d - 1, zb).wait_recv)
                if d < nz - 1:
                    go(both_conds(cond, can[way]), zcopy(way, j, d, zb))
                spread(cond, j, slot, zb)
                go(cond, ccopy(c, j, 0, slot, x, zb))
            x_arrivals(d - 1, j)
    for j in range(C_IN):
        x_arrivals(nz - 1, j)

    mt = min(LANES, total)
    nt = min(256, ff)
    for j in range(C_IN):
        for d in range(nz):
            for cond, slot, zb in slots(d):
                for xd in range(0 if d else 1, nx):
                    cp = ccopy(other, j, xd, slot, lax.rem(x + nx - xd, nx), zb)
                    if cond is None:
                        cp.wait_recv()
                    else:
                        pl.when(cond)(cp.wait_recv)
        for h in range(2):
            k = h * C_IN + j
            for i in range(2):
                w_copy(i, k).wait()

            def tile(i, carry, k=k, first=(j == 0 and h == 0)):
                n = al((i % (ff // nt)) * nt, nt)
                m = al((i // (ff // nt)) * mt, mt)
                left = gat[k, pl.ds(m, mt), :]
                for w, acc in ((wg, acc_g), (wu, acc_u)):
                    v = jnp.dot(left, w[pl.ds(k * wi, wi), pl.ds(n, nt)], preferred_element_type=F32)
                    if first:
                        acc[pl.ds(m, mt), pl.ds(n, nt)] = v
                    else:
                        acc[pl.ds(m, mt), pl.ds(n, nt)] += v
                return carry
            lax.fori_loop(0, (ff // nt) * (total // mt), tile, 0)

    for n, xb, zb in chips():
        dx, dz = (n + 1) // nz, (n + 1) % nz
        p = gts.at[rows_of(lax.rem(x + nx - dx, nx), lax.rem(z + nz - dz, nz)), :]
        rc(p, p, gts_s.at[n], gts_r.at[n], grp=xb * 2 + c, loc=zb).wait_recv()

    def hidden_tile(i, carry):
        m = al(i * mt, mt)
        v = acc_g[pl.ds(m, mt), :]
        hid[pl.ds(m, mt), :] = (v / (1.0 + jnp.exp(-v)) * acc_u[pl.ds(m, mt), :]).astype(BF16)
        return carry
    lax.fori_loop(0, total // mt, hidden_tile, 0)

    expert = (g * nz + z) // (nz // EXP_GROUP)

    def down(h, j, m):
        y = jnp.dot(hid[pl.ds(m, mt), :], wd[h * C_OUT + j], preferred_element_type=F32)
        at = lax.broadcasted_iota(jnp.int32, (mt, LANES), 1)
        w = jnp.where(at == expert, gts[pl.ds(m, mt), :].astype(F32), 0.0)
        return y * jnp.sum(w, axis=1, keepdims=True)

    def core_out(j):
        return rc(snd.at[j], tin.at[j], ss.at[j], sr.at[j], grp=mate)

    span = nz * blk

    def x_out(j, xd, to):
        return rc(tin.at[j, pl.ds(al(to * span, span), span), :], xin.at[j, xd - 1],
                  xos.at[j, xd - 1], xor.at[j, xd - 1], grp=to * 2 + c)

    def down_other(j):
        wd_copy(other, j).wait()

        def tile(i, carry):
            m = al(i * mt, mt)
            snd[j, pl.ds(m, mt), :] = down(other, j, m).astype(BF16)
            return carry
        lax.fori_loop(0, total // mt, tile, 0)
        core_out(j).start()

    def down_own(j):
        wd_copy(c, j).wait()
        core_out(j).wait_recv()

        def tile(i, carry):
            m = al(i * mt, mt)
            tin[j, pl.ds(m, mt), :] = (down(c, j, m) + tin[j, pl.ds(m, mt), :].astype(F32)).astype(BF16)
            return carry
        lax.fori_loop(0, total // mt, tile, 0)
        for xd in range(1, nx):
            go(None, x_out(j, xd, lax.rem(x + xd, nx)))

    down_other(0)
    for j in range(C_OUT):
        if j + 1 < C_OUT:
            down_other(j + 1)
        down_own(j)

    def z_out(way, j, t):
        src, dst = ((zsr, zl), (zsl, zr))[way]
        return rc(src.at[j, t - 1], dst.at[j, t - 1], zos.at[way, j, t - 1], zor.at[way, j, t - 1],
                  loc=z + 1 if way == 0 else z - 1)

    for j in range(C_OUT):
        for xd in range(1, nx):
            x_out(j, xd, x).wait_recv()

        def q(zb):
            v = tin[j, rows_of(x, zb), :].astype(F32)
            for xd in range(1, nx):
                v = v + xin[j, xd - 1, pl.ds(al(zb * blk, blk), blk), :].astype(F32)
            return v

        for t in range(nz - 1, 0, -1):
            for way in range(2):
                buf, into = ((zsr, zl), (zsl, zr))[way]
                zb = z + t if way == 0 else z - t
                reach = z + t < nz if way == 0 else z >= t
                edge = z == 0 if way == 0 else z == nz - 1

                @pl.when(jnp.logical_and(reach, edge))
                def _():
                    buf[j, t - 1] = q(zb).astype(BF16)
                if t < nz - 1:
                    @pl.when(jnp.logical_and(reach, jnp.logical_not(edge)))
                    def _():
                        z_out(way, j, t + 1).wait_recv()
                        buf[j, t - 1] = (q(zb) + into[j, t].astype(F32)).astype(BF16)
                go(reach, z_out(way, j, t))
        res[...] = q(z)
        for way in range(2):
            into = (zl, zr)[way]

            @pl.when(can[1 - way])
            def _():
                z_out(way, j, 1).wait_recv()
                res[...] += into[j, 0].astype(F32)
        v = res[...]
        fin[j] = v.astype(BF16)
        go(None, rc(fin.at[j], fin_in.at[j], fs.at[j], fr.at[j], grp=mate))
        out_ref[:, pl.ds(al(c * half + j * wo, LANES), wo)] = jnp.where(c == 0, v[:rows], v[rows:]).astype(BF16)

    for j in range(C_OUT):
        rc(fin.at[j], fin_in.at[j], fs.at[j], fr.at[j], grp=mate).wait_recv()
        v = fin_in[j].astype(F32)
        out_ref[:, pl.ds(al(other * half + j * wo, LANES), wo)] = jnp.where(c == 0, v[:rows], v[rows:]).astype(BF16)

    swap.wait_send()
    for j in range(C_OUT):
        core_out(j).wait_send()
    for cond, cp in sends:
        if cond is None:
            cp.wait_send()
        else:
            pl.when(cond)(cp.wait_send)


def body(tokens, expert_ids, gate_values, w_gate, w_up, w_down):
    rows, width = tokens.shape
    nx = lax.axis_size("grp") // 2
    nz = lax.axis_size("loc")
    half = width // 2
    blk = 2 * rows
    total = nx * nz * blk
    ff = w_gate.shape[2]
    wi, wo = half // C_IN, half // C_OUT
    dma = pltpu.SemaphoreType.DMA
    ns = 2 * nz - 1
    vm = pltpu.VMEM
    scratch = [
        vm((width, ff), BF16), vm((width, ff), BF16), vm((2 * C_OUT, ff, wo), BF16),
        vm((blk, half + LANES), BF16), vm((blk, half + LANES), BF16),
        vm((2 * C_IN, total, wi), BF16), vm((total, LANES), BF16),
        vm((total, ff), F32), vm((total, ff), F32), vm((total, ff), BF16),
        vm((C_OUT, total, wo), BF16), vm((C_OUT, total, wo), BF16),
        vm((C_OUT, nx - 1, nz * blk, wo), BF16),
        vm((C_OUT, nz - 1, blk, wo), BF16), vm((C_OUT, nz - 1, blk, wo), BF16),
        vm((C_OUT, nz - 1, blk, wo), BF16), vm((C_OUT, nz - 1, blk, wo), BF16),
        vm((blk, wo), F32), vm((C_OUT, blk, wo), BF16), vm((C_OUT, blk, wo), BF16),
        dma((2, 2 * C_IN)), dma((2 * C_OUT,)), dma((2,)), dma((nx * nz - 1,)), dma((nx * nz - 1,)),
        dma((2, C_IN, nz - 1)), dma((2, C_IN, nz - 1)),
        dma((C_IN, nx - 1, ns)), dma((C_IN, nx - 1, ns)),
        dma((C_IN, nx, ns)), dma((C_IN, nx, ns)),
        dma((C_OUT,)), dma((C_OUT,)), dma((C_OUT, nx - 1)), dma((C_OUT, nx - 1)),
        dma((2, C_OUT, nz - 1)), dma((2, C_OUT, nz - 1)), dma((C_OUT,)), dma((C_OUT,)),
    ]
    inside = pl.BlockSpec(memory_space=pltpu.VMEM)
    outside = pl.BlockSpec(memory_space=pl.ANY)
    return pl.pallas_call(
        functools.partial(kernel, nx, nz),
        out_shape=jax.ShapeDtypeStruct((rows, width), BF16),
        in_specs=[inside] * 3 + [outside] * 3,
        out_specs=inside,
        scratch_shapes=scratch,
        compiler_params=pltpu.CompilerParams(
            collective_id=0, has_side_effects=True, vmem_limit_bytes=63 * 1024 * 1024),
    )(tokens, expert_ids, gate_values, w_gate, w_up, w_down)


def solution(mesh):
    placed = (
        P(("rep", "grp", "loc"), None),
        P(("rep", "grp", "loc"), None),
        P(("rep", "grp", "loc"), None),
        P(("grp", "loc"), None, None),
        P(("grp", "loc"), None, None),
        P(("grp", "loc"), None, None),
    )
    return jax.shard_map(
        body, mesh=mesh, in_specs=placed, out_specs=P(("rep", "grp", "loc"), None), check_vma=False
    )
```

time: 125 us -> 77.1 us (0.62)
  Pallas kernels: 0 us -> 75.3 us
  waiting for transfers between devices: 38.8 us -> 0 us
  blocking collectives: 24.9 us -> 0 us
  matrix products: 23 us -> 0 us
  starting transfers between devices: 20 us -> 0 us
  other arithmetic: 8.54 us -> 0 us
  local copies, waits for them, and re-layouts: 9.48 us -> 1.55 us
    pallas_call x0 -> x1, Pallas kernels: none -> 75.3 us  [body(): pl.pallas_call(functools.partial(kernel, nx, nz), out_shape=jax.ShapeDtyp...]
    all_to_all x5 -> x0, waiting for transfers between devices: 38.8 us -> none  [the longest x1 21.4 us: body(): lax.all_to_all(fwd_rows, 'loc', split_axis=0, concat_axis=0, tiled=True)]
    all_to_all x1 -> x0, blocking collectives: 24.9 us -> none  [body(): lax.all_to_all(outputs, 'loc', split_axis=0, concat_axis=0, tiled=True)]
    dot_general x4 -> x0, matrix products: 23 us -> none  [the longest x1 14.6 us: expert_rows(): down = jnp.dot(hidden, w_down[0], preferred_element_type=jnp.float32)]
    all_to_all x5 -> x0, starting transfers between devices: 20 us -> none  [the longest x1 5.33 us: body(): lax.all_to_all(fwd_gates, 'loc', split_axis=0, concat_axis=0, tiled=True)]
    gather x6 -> x0, local copies, waits for them, and re-layouts: 4.46 us -> none  [the longest x1 1.12 us: body(): flat_arrived[safe_two]]
    scatter-add x1 -> x0, other arithmetic: 3.06 us -> none  [body(): partial_value = jnp.zeros((n_grp * rows, width), jnp.float32).at[safe_two...]
    select_n x8 -> x0, other arithmetic: 2.77 us -> none  [the longest x1 1.06 us: body(): jnp.where(valid_two[:, None], flat_arrived[safe_two], jnp.zeros((), jnp.b...]
  transfers between devices with their start and end apart: 5 -> 0, of which waited for: 5 -> 0; matrix products, arithmetic and copies ran while one was open for 6% -> 0% of each run, Pallas kernels for 0% -> 0%
where the time goes in v1:
time: 77.1 us; the launch traced here: 76.9 us
  Pallas kernels  75.3 us (98%)
  local copies, waits for them, and re-layouts  1.55 us (2%)
    pallas_call x1, Pallas kernels, body(): pl.pallas_call(functools.partial(kernel, nx, nz), out_shape=jax.ShapeDtyp...  75.3 us
    unnamed x1, local copies, waits for them, and re-layouts  1.55 us

profile of v1, /device:TPU:0, one launch (start us, length us, event | category | flops | bytes accessed | tf_op | source)
XLA Modules:
  0.0 76.9 jit_solution(17032793440062761138)
XLA Ops:
  0.0 75.3 %shard_map.64 = bf16[8,7168]{1,0:T(8,128)(2,1)} custom-call(bf16[8,7168]{1,0:T(8,128)(2,1)} %tok_ref.1, s32[8,8]{1,0:T(8,128)} %ids_ref.1, bf16[8,8]{1,0:T(8,128)(2,1)} %gv_ref.1, bf16[1,7168,1024]{2,1,0:T(8,128)(2,1)} %wg_hbm.1, bf16[1,7168,1024]{2,1,0:T(8,128)(2,1)} %wu_hbm.1, bf16[1,1024,7168]{2,1,0:T(8,128)(2,1)} %wd_hbm.1), custom_call_target="tpu_custom_call" | custom-call | tf_op jit(solution)/shard_map/pallas_call | solution.py:350
  75.3 1.6 %copy.8 = bf16[8,7168]{1,0:T(8,128)(2,1)} copy(bf16[8,7168]{1,0:T(8,128)(2,1)} %shard_map.64) | data formatting | bytes 229376

commit v2 on v1

--- a/solution.py
+++ b/solution.py
@@ -20,7 +20,7 @@
 
 
 def kernel(nx, nz, tok_ref, ids_ref, gv_ref, wg_hbm, wu_hbm, wd_hbm, out_ref,
-           wg, wu, wd, pk, pk_in, gat, gts, acc_g, acc_u, hid, snd, tin, xin, zl, zr, zsl, zsr, res, fin, fin_in,
+           wg, wu, wd, pk, pk_in, gat, gts, acc_g, acc_u, hid, snd, tin, xin, zout, zin, res, fin, fin_in,
            w_sem, wd_sem, pk_sem, gts_s, gts_r, zs, zv, xs, xv, cs, cv, ss, sr, xos, xor, zos, zor, fs, fr):
     rows, width = tok_ref.shape
     half = width // 2
@@ -108,15 +108,12 @@
         else:
             pl.when(cond)(cp.start)
 
-    def both_conds(p, q):
-        return p if q is None else q if p is None else jnp.logical_and(p, q)
-
     def piece(h, j, xb, zb):
         return gat.at[h * C_IN + j, rows_of(xb, zb), :]
 
-    def zcopy(way, j, d, zb):
+    def zcopy(way, j, d, zb, to):
         p = piece(c, j, x, zb)
-        return rc(p, p, zs.at[way, j, d], zv.at[way, j, d], loc=z + 1 if way == 0 else z - 1)
+        return rc(p, p, zs.at[way, j, d - 1], zv.at[way, j, d - 1], loc=to)
 
     def xcopy(j, xd, slot, xb, zb, to):
         p = piece(c, j, xb, zb)
@@ -126,16 +123,19 @@
         p = piece(h, j, xb, zb)
         return rc(p, p, cs.at[j, xd, slot], cv.at[j, xd, slot], grp=mate)
 
-    can = (z + 1 < nz, z >= 1)
+    def reach(way, d):
+        return z + d < nz if way == 0 else z >= d
 
     def spread(cond, j, slot, zb):
         for xd in range(1, nx):
             go(cond, xcopy(j, xd, slot, x, zb, lax.rem(x + xd, nx)))
 
-    for j in range(C_IN):
-        for way in range(2):
-            go(can[way], zcopy(way, j, 0, z))
-        spread(None, j, 0, z)
+    for d in range(1, nz):
+        for j in range(C_IN):
+            for way in range(2):
+                go(reach(way, d), zcopy(way, j, d, z, z + d if way == 0 else z - d))
+            if d == 1:
+                spread(None, j, 0, z)
     for n, xb, zb in chips():
         p = gts.at[rows_of(x, z), :]
         go(None, rc(p, p, gts_s.at[n], gts_r.at[n], grp=xb * 2 + c, loc=zb))
@@ -162,9 +162,7 @@
     for d in range(1, nz):
         for j in range(C_IN):
             for way, (cond, slot, zb) in enumerate(slots(d)):
-                pl.when(cond)(zcopy(way, j, d - 1, zb).wait_recv)
-                if d < nz - 1:
-                    go(both_conds(cond, can[way]), zcopy(way, j, d, zb))
+                pl.when(cond)(zcopy(way, j, d, zb, z).wait_recv)
                 spread(cond, j, slot, zb)
                 go(cond, ccopy(c, j, 0, slot, x, zb))
             x_arrivals(d - 1, j)
@@ -257,12 +255,10 @@
             down_other(j + 1)
         down_own(j)
 
-    def z_out(way, j, t):
-        src, dst = ((zsr, zl), (zsl, zr))[way]
-        return rc(src.at[j, t - 1], dst.at[j, t - 1], zos.at[way, j, t - 1], zor.at[way, j, t - 1],
-                  loc=z + 1 if way == 0 else z - 1)
-
-    for j in range(C_OUT):
+    def z_out(way, j, d, to):
+        return rc(zout.at[j, to], zin.at[way, j, d - 1], zos.at[way, j, d - 1], zor.at[way, j, d - 1], loc=to)
+
+    def sum_x(j):
         for xd in range(1, nx):
             x_out(j, xd, x).wait_recv()
 
@@ -272,34 +268,33 @@
                 v = v + xin[j, xd - 1, pl.ds(al(zb * blk, blk), blk), :].astype(F32)
             return v
 
-        for t in range(nz - 1, 0, -1):
+        for d in range(nz - 1, 0, -1):
             for way in range(2):
-                buf, into = ((zsr, zl), (zsl, zr))[way]
-                zb = z + t if way == 0 else z - t
-                reach = z + t < nz if way == 0 else z >= t
-                edge = z == 0 if way == 0 else z == nz - 1
-
-                @pl.when(jnp.logical_and(reach, edge))
+                zb = z + d if way == 0 else z - d
+
+                @pl.when(reach(way, d))
                 def _():
-                    buf[j, t - 1] = q(zb).astype(BF16)
-                if t < nz - 1:
-                    @pl.when(jnp.logical_and(reach, jnp.logical_not(edge)))
-                    def _():
-                        z_out(way, j, t + 1).wait_recv()
-                        buf[j, t - 1] = (q(zb) + into[j, t].astype(F32)).astype(BF16)
-                go(reach, z_out(way, j, t))
-        res[...] = q(z)
-        for way in range(2):
-            into = (zl, zr)[way]
-
-            @pl.when(can[1 - way])
-            def _():
-                z_out(way, j, 1).wait_recv()
-                res[...] += into[j, 0].astype(F32)
-        v = res[...]
+                    zout[j, zb] = q(zb).astype(BF16)
+                go(reach(way, d), z_out(way, j, d, zb))
+        res[j] = q(z)
+
+    def sum_z(j):
+        for d in range(1, nz):
+            for way in range(2):
+                @pl.when(reach(1 - way, d))
+                def _():
+                    z_out(way, j, d, z).wait_recv()
+                    res[j] += zin[way, j, d - 1].astype(F32)
+        v = res[j]
         fin[j] = v.astype(BF16)
         go(None, rc(fin.at[j], fin_in.at[j], fs.at[j], fr.at[j], grp=mate))
         out_ref[:, pl.ds(al(c * half + j * wo, LANES), wo)] = jnp.where(c == 0, v[:rows], v[rows:]).astype(BF16)
+
+    for j in range(C_OUT):
+        sum_x(j)
+        if j:
+            sum_z(j - 1)
+    sum_z(C_OUT - 1)
 
     for j in range(C_OUT):
         rc(fin.at[j], fin_in.at[j], fs.at[j], fr.at[j], grp=mate).wait_recv()
@@ -335,9 +330,8 @@
         vm((total, ff), F32), vm((total, ff), F32), vm((total, ff), BF16),
         vm((C_OUT, total, wo), BF16), vm((C_OUT, total, wo), BF16),
         vm((C_OUT, nx - 1, nz * blk, wo), BF16),
-        vm((C_OUT, nz - 1, blk, wo), BF16), vm((C_OUT, nz - 1, blk, wo), BF16),
-        vm((C_OUT, nz - 1, blk, wo), BF16), vm((C_OUT, nz - 1, blk, wo), BF16),
-        vm((blk, wo), F32), vm((C_OUT, blk, wo), BF16), vm((C_OUT, blk, wo), BF16),
+        vm((C_OUT, nz, blk, wo), BF16), vm((2, C_OUT, nz - 1, blk, wo), BF16),
+        vm((C_OUT, blk, wo), F32), vm((C_OUT, blk, wo), BF16), vm((C_OUT, blk, wo), BF16),
         dma((2, 2 * C_IN)), dma((2 * C_OUT,)), dma((2,)), dma((nx * nz - 1,)), dma((nx * nz - 1,)),
         dma((2, C_IN, nz - 1)), dma((2, C_IN, nz - 1)),
         dma((C_IN, nx - 1, ns)), dma((C_IN, nx - 1, ns)),

time: 77.1 us -> 56.3 us (0.73)
  Pallas kernels: 75.3 us -> 54.6 us
    pallas_call x1, Pallas kernels: 75.3 us -> 54.6 us  [body(): pl.pallas_call(functools.partial(kernel, nx, nz), out_shape=jax.ShapeDtyp...]
where the time goes in v2:
time: 56.3 us; the launch traced here: 56.1 us
  Pallas kernels  54.6 us (97%)
  local copies, waits for them, and re-layouts  1.55 us (3%)
    pallas_call x1, Pallas kernels, body(): pl.pallas_call(functools.partial(kernel, nx, nz), out_shape=jax.ShapeDtyp...  54.6 us
    unnamed x1, local copies, waits for them, and re-layouts  1.55 us

profile of v2, /device:TPU:0, one launch (start us, length us, event | category | flops | bytes accessed | tf_op | source)
XLA Modules:
  0.0 56.1 jit_solution(12694865097981411378)
XLA Ops:
  0.0 54.6 %shard_map.64 = bf16[8,7168]{1,0:T(8,128)(2,1)} custom-call(bf16[8,7168]{1,0:T(8,128)(2,1)} %tok_ref.1, s32[8,8]{1,0:T(8,128)} %ids_ref.1, bf16[8,8]{1,0:T(8,128)(2,1)} %gv_ref.1, bf16[1,7168,1024]{2,1,0:T(8,128)(2,1)} %wg_hbm.1, bf16[1,7168,1024]{2,1,0:T(8,128)(2,1)} %wu_hbm.1, bf16[1,1024,7168]{2,1,0:T(8,128)(2,1)} %wd_hbm.1), custom_call_target="tpu_custom_call" | custom-call | tf_op jit(solution)/shard_map/pallas_call | solution.py:344
  54.6 1.6 %copy.8 = bf16[8,7168]{1,0:T(8,128)(2,1)} copy(bf16[8,7168]{1,0:T(8,128)(2,1)} %shard_map.64) | data formatting | bytes 229376

commit v3 on v2

--- a/solution.py
+++ b/solution.py
@@ -108,12 +108,15 @@
         else:
             pl.when(cond)(cp.start)
 
+    def both_conds(p, q):
+        return p if q is None else q if p is None else jnp.logical_and(p, q)
+
     def piece(h, j, xb, zb):
         return gat.at[h * C_IN + j, rows_of(xb, zb), :]
 
-    def zcopy(way, j, d, zb, to):
+    def zcopy(way, j, d, zb):
         p = piece(c, j, x, zb)
-        return rc(p, p, zs.at[way, j, d - 1], zv.at[way, j, d - 1], loc=to)
+        return rc(p, p, zs.at[way, j, d], zv.at[way, j, d], loc=z + 1 if way == 0 else z - 1)
 
     def xcopy(j, xd, slot, xb, zb, to):
         p = piece(c, j, xb, zb)
@@ -123,19 +126,16 @@
         p = piece(h, j, xb, zb)
         return rc(p, p, cs.at[j, xd, slot], cv.at[j, xd, slot], grp=mate)
 
-    def reach(way, d):
-        return z + d < nz if way == 0 else z >= d
+    can = (z + 1 < nz, z >= 1)
 
     def spread(cond, j, slot, zb):
         for xd in range(1, nx):
             go(cond, xcopy(j, xd, slot, x, zb, lax.rem(x + xd, nx)))
 
-    for d in range(1, nz):
-        for j in range(C_IN):
-            for way in range(2):
-                go(reach(way, d), zcopy(way, j, d, z, z + d if way == 0 else z - d))
-            if d == 1:
-                spread(None, j, 0, z)
+    for j in range(C_IN):
+        for way in range(2):
+            go(can[way], zcopy(way, j, 0, z))
+        spread(None, j, 0, z)
     for n, xb, zb in chips():
         p = gts.at[rows_of(x, z), :]
         go(None, rc(p, p, gts_s.at[n], gts_r.at[n], grp=xb * 2 + c, loc=zb))
@@ -162,7 +162,9 @@
     for d in range(1, nz):
         for j in range(C_IN):
             for way, (cond, slot, zb) in enumerate(slots(d)):
-                pl.when(cond)(zcopy(way, j, d, zb, z).wait_recv)
+                pl.when(cond)(zcopy(way, j, d - 1, zb).wait_recv)
+                if d < nz - 1:
+                    go(both_conds(cond, can[way]), zcopy(way, j, d, zb))
                 spread(cond, j, slot, zb)
                 go(cond, ccopy(c, j, 0, slot, x, zb))
             x_arrivals(d - 1, j)
@@ -257,6 +259,9 @@
 
     def z_out(way, j, d, to):
         return rc(zout.at[j, to], zin.at[way, j, d - 1], zos.at[way, j, d - 1], zor.at[way, j, d - 1], loc=to)
+
+    def reach(way, d):
+        return z + d < nz if way == 0 else z >= d
 
     def sum_x(j):
         for xd in range(1, nx):

time: 56.3 us -> 53 us (0.941)
  Pallas kernels: 54.6 us -> 51.3 us
    pallas_call x1, Pallas kernels: 54.6 us -> 51.3 us  [body(): pl.pallas_call(functools.partial(kernel, nx, nz), out_shape=jax.ShapeDtyp...]
where the time goes in v3:
time: 53 us; the launch traced here: 52.8 us
  Pallas kernels  51.3 us (97%)
  local copies, waits for them, and re-layouts  1.55 us (3%)
    pallas_call x1, Pallas kernels, body(): pl.pallas_call(functools.partial(kernel, nx, nz), out_shape=jax.ShapeDtyp...  51.3 us
    unnamed x1, local copies, waits for them, and re-layouts  1.55 us

profile of v3, /device:TPU:0, one launch (start us, length us, event | category | flops | bytes accessed | tf_op | source)
XLA Modules:
  0.0 52.8 jit_solution(850103191804497786)
XLA Ops:
  0.0 51.3 %shard_map.64 = bf16[8,7168]{1,0:T(8,128)(2,1)} custom-call(bf16[8,7168]{1,0:T(8,128)(2,1)} %tok_ref.1, s32[8,8]{1,0:T(8,128)} %ids_ref.1, bf16[8,8]{1,0:T(8,128)(2,1)} %gv_ref.1, bf16[1,7168,1024]{2,1,0:T(8,128)(2,1)} %wg_hbm.1, bf16[1,7168,1024]{2,1,0:T(8,128)(2,1)} %wu_hbm.1, bf16[1,1024,7168]{2,1,0:T(8,128)(2,1)} %wd_hbm.1), custom_call_target="tpu_custom_call" | custom-call | tf_op jit(solution)/shard_map/pallas_call | solution.py:349
  51.3 1.6 %copy.8 = bf16[8,7168]{1,0:T(8,128)(2,1)} copy(bf16[8,7168]{1,0:T(8,128)(2,1)} %shard_map.64) | data formatting | bytes 229376
